TPU v7x, 256 devices: a whole 4x4x8 slice. The times are simulated.
256 devices in a mesh: vox: 8 (over x, core), mem: 32 (over y, z).
Axes of the slice: x: 4, y: 4, z: 8, core: 2. Of those that a mesh axis runs over, the one named last changes fastest.
Arguments:
- ensemble: bfloat16 [256, 524288], P('mem', 'vox'), may hold values from -6 to 6
- partials: float32 [8, 256, 131072], P('vox', 'mem'), may hold values from -6 to 6
- perturb: float32 [256, 131072], P('mem', 'vox'), may hold values from -6 to 6
- observed: float32 [131072], P('vox'), may hold values from -6 to 6
- variance: float32 [131072], P('vox'), may hold values from 0.5 to 2
- obs_lists: int32 [4096, 64], P(('vox', 'mem')), may hold values from 0 to 127, all different within a row
- taper_index: int32 [4096, 64], P(('vox', 'mem')), may hold values from 0 to 15
- taper_table: float32 [16], replicated, may hold values from 0.1 to 1
Outputs:
- updated: bfloat16 [256, 524288], P('mem', 'vox')
All inputs are finite; a program needn't handle non-finite values.
Results may differ from a plain program's by a relative error of at most 0.017.
Values may be sent and summed in bfloat16 or wider, within the bound.
A program may use at most 128 MiB of HBM per device.

v0:
```python
import jax
import jax.numpy as jnp
from jax import lax
from jax.sharding import PartitionSpec as P

OB = 128


def center(values):
    as_float = values.astype(jnp.float32)
    return (as_float - jnp.mean(as_float, axis=0, keepdims=True)).astype(jnp.bfloat16)


def block_moments(obs_anom, weights):
    return jnp.einsum("kbi,lbi->bkl", obs_anom, weights, preferred_element_type=jnp.float32)


def from_moments(moments, coeff, state_anom):
    high = lax.Precision.HIGHEST
    combined = jnp.einsum("bo,okl->bkl", coeff, moments, precision=high).astype(jnp.bfloat16)
    return jnp.einsum("kbc,bkl->lbc", state_anom, combined, preferred_element_type=jnp.float32)


def local(ensemble, partials, perturb, observed, variance, obs_lists, taper_index, taper_table):
    summed = lax.psum_scatter(
        partials[0].astype(jnp.bfloat16), "vox", scatter_dimension=1, tiled=True
    )
    weights = (
        (observed[None, :] + perturb - summed.astype(jnp.float32)) / variance[None, :]
    ).astype(jnp.bfloat16)
    members = lax.all_to_all(ensemble, "mem", split_axis=1, concat_axis=0, tiled=True)
    count = members.shape[0]
    blocks = obs_lists.shape[0]
    cells = members.shape[1] // blocks
    groups = weights.shape[1] // OB
    state_anom = center(members).reshape(count, blocks, cells)
    table_hits = (
        taper_index[:, :, None] == jnp.arange(taper_table.shape[0], dtype=jnp.int32)[None, None, :]
    ).astype(jnp.float32)
    tapers = jnp.sum(table_hits * taper_table[None, None, :], axis=2)
    picks = (obs_lists[:, :, None] == jnp.arange(groups, dtype=jnp.int32)[None, None, :]).astype(
        jnp.float32
    )
    coeff = jnp.sum(tapers[:, :, None] * picks, axis=1)
    pred_all, wts_all = (
        lax.all_gather(summed, "mem", axis=0, tiled=True),
        lax.all_gather(weights, "mem", axis=0, tiled=True),
    )
    obs_anom = center(pred_all).reshape(count, groups, OB)
    moments = block_moments(obs_anom, wts_all.reshape(count, groups, OB))
    increment = from_moments(moments, coeff, state_anom).reshape(count, blocks * cells)
    updated = (members.astype(jnp.float32) + increment * (1.0 / (count - 1))).astype(jnp.bfloat16)
    return lax.all_to_all(updated, "mem", split_axis=0, concat_axis=1, tiled=True)


def solution(mesh):
    return jax.shard_map(
        local,
        mesh=mesh,
        in_specs=(
            P("mem", "vox"),
            P("vox", "mem", None),
            P("mem", "vox"),
            P("vox"),
            P("vox"),
            P(("vox", "mem"), None),
            P(("vox", "mem"), None),
            P(),
        ),
        out_specs=P("mem", "vox"),
        check_vma=False,
    )
```

profile of v0, /device:TPU:1, one launch (start us, length us, event | category | flops | bytes accessed | tf_op | source)
XLA Modules:
  0.0 372.6 jit_solution(18339346806040277107)
XLA Ops:
  6.5 0.0 copy-start
  6.5 0.0 copy-start.2
  6.5 0.0 copy-start.1
  6.5 0.0 reduce-scatter.2.cloned.1.call-start
  6.5 3.8 %convert_bitcast_fusion.2 = bf16[8,131072]{1,0:T(8,128)(2,1)} fusion(f32[1,8,131072]{2,1,0:T(8,128)} %param.9), kind=kLoop, calls=%fused_computation.19 | loop fusion | flops 1048576 | bytes 6291456 | tf_op jit(solution)/shard_map/convert_element_type | solution.py:26
  10.3 0.0 copy-start.4
  10.3 0.0 copy-start.5
  10.3 0.0 copy-start.3
  10.3 0.0 reduce-scatter.2.cloned.1.call-update
  10.4 0.0 all-gather.3.cloned.1.call-start
  10.4 37.5 %reduce-scatter.2.cloned.1.call-done = bf16[8,16384]{1,0:T(8,128)(2,1)} async-done(((bf16[8,131072]{1,0:T(8,128)(2,1)}), bf16[8,16384]{1,0:T(8,128)(2,1)}) %reduce-scatter.2.cloned.1.call-update) | async-done | bytes 262160 | tf_op jit(solution)/shard_map/reduce_scatter | solution.py:25
  47.9 0.0 all-gather.3.cloned.1.call-update
  47.9 0.0 all-gather.5.cloned.1.call-start
  48.0 0.0 copy-done
  48.0 0.0 copy-done.2
  48.0 0.0 copy-done.1
  48.0 1.8 divide_convert_fusion
  49.8 0.0 all-gather.5.cloned.1.call-update
  49.8 9.3 %all-to-all-start = ((bf16[8,32,2048]{2,0,1:T(8,128)(2,1)}), bf16[8,32,2048]{2,0,1:T(8,128)(2,1)S(1)}, u32[]{:S(2)}, u32[]{:S(2)}) async-start(bf16[8,32,2048]{2,0,1:T(8,128)(2,1)} %bitcast), calls=%async_computation | async-start | bytes 2097152 | tf_op jit(solution)/shard_map/all_to_all | solution.py:31
  59.1 0.0 copy-done.4
  59.1 0.0 copy-done.5
  59.2 0.1 select_reduce_fusion.1
  59.3 0.0 copy-done.3
  59.3 0.3 select_reduce_fusion
  59.6 24.6 %all-to-all-done = bf16[8,32,2048]{2,0,1:T(8,128)(2,1)S(1)} async-done(((bf16[8,32,2048]{2,0,1:T(8,128)(2,1)}), bf16[8,32,2048]{2,0,1:T(8,128)(2,1)S(1)}, u32[]{:S(2)}, u32[]{:S(2)}) %all-to-all-start) | async-done | bytes 1048608 | tf_op jit(solution)/shard_map/all_to_all | solution.py:31
  84.2 0.2 convert_bitcast_fusion
  84.5 0.4 copy.36
  84.9 0.2 convert_reduce_fusion.1
  85.0 0.2 fusion.9
  85.2 72.3 %all-gather.3.cloned.1.call-done = bf16[256,16384]{1,0:T(8,128)(2,1)} async-done(((bf16[8,16384]{1,0:T(8,128)(2,1)}), bf16[256,16384]{1,0:T(8,128)(2,1)}) %all-gather.3.cloned.1.call-update) | async-done | bytes 8388624 | tf_op jit(solution)/shard_map/all_gather | solution.py:46
  157.5 4.8 %convert_reduce_fusion = f32[16384]{0:T(1024)S(1)} fusion(bf16[256,16384]{1,0:T(8,128)(2,1)} %all-gather.3.cloned.1.call-done), kind=kLoop, calls=%fused_computation.3 | loop fusion | flops 8372224 | bytes 8454144 | tf_op jit(solution)/shard_map/reduce_sum | solution.py:11
  162.3 93.4 %all-gather.5.cloned.1.call-done = bf16[256,16384]{1,0:T(8,128)(2,1)} async-done(((bf16[8,16384]{1,0:T(8,128)(2,1)}), bf16[256,16384]{1,0:T(8,128)(2,1)}) %all-gather.5.cloned.1.call-update) | async-done | bytes 8388624 | tf_op jit(solution)/shard_map/all_gather | solution.py:47
  255.7 11.9 %copy.27 = bf16[256,16384]{0,1:T(8,128)(2,1)} copy(bf16[256,16384]{1,0:T(8,128)(2,1)} %all-gather.5.cloned.1.call-done) | data formatting | bytes 16777216 | tf_op jit(solution)/shard_map/all_gather | solution.py:47
  267.6 17.8 %fusion.4 = f32[128,256,256]{2,1,0:T(8,128)} fusion(bf16[256,128,128]{0,2,1:T(8,128)(2,1)} %bitcast.35, bf16[256,16384]{1,0:T(8,128)(2,1)} %all-gather.3.cloned.1.call-done, f32[16384]{0:T(1024)S(1)} %broadcast_multiply_fusion), kind=kOutput, calls=%fused_computation.6 | convolution fusion | flops 2160066560 | bytes 50397184 | tf_op jit(solution)/shard_map/kbi,lbi->bkl/dot_general | solution.py:15
  285.4 43.5 %fusion.12 = bf16[16,256,256]{2,0,1:T(8,128)(2,1)S(1)} fusion(f32[128,256,256]{2,1,0:T(8,128)} %fusion.4, f32[16,128]{1,0:T(8,128)S(1)} %select_reduce_fusion), kind=kOutput, calls=%fused_computation.20 | convolution fusion | flops 1611661312 | bytes 35659776 | tf_op jit(solution)/shard_map/bo,okl->bkl/dot_general | solution.py:20
  328.9 1.7 multiply_bitcast_fusion
  330.6 2.6 copy.33
  333.1 1.7 mul.36
  334.8 0.3 fusion.8
  335.1 30.0 %all_to_all.29 = bf16[32,8,2048]{2,1,0:T(8,128)(2,1)S(1)} all-to-all(bf16[32,8,2048]{2,1,0:T(8,128)(2,1)S(1)} %fusion.8), channel_id=1, replica_groups=mesh['vox'=8,'mem'=32] {'mem'}, dimensions={0} | all-to-all | bytes 2097152 | tf_op jit(solution)/shard_map/all_to_all | solution.py:53
  365.1 1.0 copy.52
  (2 shorter events, 0.0 us)
Async XLA Ops:
  6.5 41.5 %copy-start = (f32[8,16384]{1,0:T(8,128)S(1)}, f32[8,16384]{1,0:T(8,128)}, u32[]{:S(2)}) copy-start(f32[8,16384]{1,0:T(8,128)} %param.10) | copy-start | bytes 1572868
  6.5 41.5 %copy-start.2 = (f32[16384]{0:T(1024)S(1)}, f32[16384]{0:T(1024)}, u32[]{:S(2)}) copy-start(f32[16384]{0:T(1024)} %param.11) | copy-start | bytes 196612
  6.5 41.5 %copy-start.1 = (f32[16384]{0:T(1024)S(1)}, f32[16384]{0:T(1024)}, u32[]{:S(2)}) copy-start(f32[16384]{0:T(1024)} %param.12) | copy-start | bytes 196612
  6.5 41.4 %reduce-scatter.2.cloned.1.call-start = ((), (), s32[]{:S(2)}) async-start(), calls=%async_computation.3 | async-start | bytes 2359296 | tf_op jit(solution)/shard_map/reduce_scatter | solution.py:25
  10.3 48.8 %copy-start.4 = (s32[16,64]{1,0:T(8,128)S(1)}, s32[16,64]{1,0:T(8,128)}, u32[]{:S(2)}) copy-start(s32[16,64]{1,0:T(8,128)} %param.14) | copy-start | bytes 12292
  10.3 48.8 %copy-start.5 = (f32[16]{0:T(128)S(1)}, f32[16]{0:T(128)}, u32[]{:S(2)}) copy-start(f32[16]{0:T(128)} %param.15) | copy-start | bytes 196
  10.3 48.9 %copy-start.3 = (s32[16,64]{1,0:T(8,128)S(1)}, s32[16,64]{1,0:T(8,128)}, u32[]{:S(2)}) copy-start(s32[16,64]{1,0:T(8,128)} %param.13) | copy-start | bytes 12292
  10.4 147.1 %all-gather.3.cloned.1.call-start = ((), (), s32[]{:S(2)}) async-start(), calls=%async_computation.4 | async-start | bytes 8650752 | tf_op jit(solution)/shard_map/all_gather | solution.py:46
  47.9 207.7 %all-gather.5.cloned.1.call-start = ((), (), s32[]{:S(2)}) async-start(), calls=%async_computation.5 | async-start | bytes 8650752 | tf_op jit(solution)/shard_map/all_gather | solution.py:47
  49.8 34.4 %all-to-all-start = ((bf16[8,32,2048]{2,0,1:T(8,128)(2,1)}), bf16[8,32,2048]{2,0,1:T(8,128)(2,1)S(1)}, u32[]{:S(2)}, u32[]{:S(2)}) async-start(bf16[8,32,2048]{2,0,1:T(8,128)(2,1)} %bitcast), calls=%async_computation | async-start | bytes 2097152 | tf_op jit(solution)/shard_map/all_to_all | solution.py:31
Sparse Core Ops, SparseCore 0:
  10.5 37.3 reduce-scatter.1
  50.5 106.9 all-gather.2
  160.1 95.5 all-gather.4
where the time goes:
time: 377 us; the launch traced here: 373 us
  waiting for transfers between devices  228 us (60%)
  matrix products  63 us (17%)
  blocking collectives  30 us (8%)
  local copies, waits for them, and re-layouts  17.6 us (5%)
  between operations  13.3 us (4%)
  other arithmetic  11.6 us (3%)
  starting transfers between devices  9.41 us (2%)
    all_gather x1, waiting for transfers between devices, local(): lax.all_gather(weights, 'mem', axis=0, tiled=True)  93.4 us
    all_gather x1, waiting for transfers between devices, local(): lax.all_gather(summed, 'mem', axis=0, tiled=True)  72.3 us
    dot_general x1, matrix products, from_moments(): jnp.einsum('bo,okl->bkl', coeff, moments, precision=high)  43.5 us
    reduce_scatter x1, waiting for transfers between devices, local(): lax.psum_scatter(partials[0].astype(jnp.bfloat16), 'vox', scatter_dimensi...  37.5 us
    all_to_all x1, blocking collectives, local(): lax.all_to_all(updated, 'mem', split_axis=0, concat_axis=1, tiled=True)  30 us
    all_to_all x1, waiting for transfers between devices, local(): lax.all_to_all(ensemble, 'mem', split_axis=1, concat_axis=0, tiled=True)  24.6 us
    dot_general x1, matrix products, block_moments(): jnp.einsum('kbi,lbi->bkl', obs_anom, weights, preferred_element_type=jnp....  17.8 us
    all_gather x1, local copies, waits for them, and re-layouts, local(): lax.all_gather(weights, 'mem', axis=0, tiled=True)  11.9 us
  transfers between devices with their start and end apart: 4, of which 4 were waited for; matrix products, arithmetic and copies ran while one was open for 2% of the time, Pallas kernels for 0%

commit v1 on v0

v1 whole, which is shorter than its diff:
```python
import functools

import jax
import jax.numpy as jnp
from jax import lax
from jax.experimental import pallas as pl
from jax.experimental.pallas import tpu as pltpu
from jax.sharding import PartitionSpec as P

MESH = pl.DeviceIdType.MESH
NX, NC, NY, NZ = 4, 2, 4, 8
NS = NX * NC
MEM = 8
BLK = 128
F32, BF16 = jnp.float32, jnp.bfloat16


def kernel(
    ens, par, per, obs, var, coef, out,
    par_v, per_v, obs_v, core_send, core_recv, rs_send, rs_recv, own_sum,
    a0, a1, a2, vh, ch, p1, p_all, x1, x_all, wt, m_f, m_all, comb, ost,
    ld_s, loc_s,
    co_ss, co_rs, rs_ss, rs_rs, x1_ss, x1_rs, a1_ss, a1_rs, v_ss, v_rs, c_ss, c_rs,
    xz_ss, xz_rs, az_ss, az_rs, pz_ss, pz_rs, py_ss, py_rs, xy_ss, xy_rs,
    mx_ss, mx_rs, mc_ss, mc_rs, o_ss, o_rs,
):
    v = lax.axis_index("vox")
    mem = lax.axis_index("mem")
    x, c = v // NC, lax.rem(v, NC)
    y, z = mem // NZ, lax.rem(mem, NZ)
    oc = 1 - c
    cells = ens.shape[1] // NS
    data = per.shape[1] // NS
    nob = data // BLK
    nvb = cells // BLK
    nl = NZ * MEM

    def dev(vox, yy, zz):
        return (vox, yy * NZ + zz)

    def rc(src, dst, ss, rs, to):
        return pltpu.make_async_remote_copy(
            src_ref=src, dst_ref=dst, send_sem=ss, recv_sem=rs, device_id=to, device_id_type=MESH
        )

    def mod(a, n):
        return lax.rem(a, n)

    loads = [
        pltpu.make_async_copy(par.at[0], par_v, ld_s.at[0]),
        pltpu.make_async_copy(per, per_v, ld_s.at[1]),
        pltpu.make_async_copy(obs, obs_v, ld_s.at[2]),
    ]
    for cp in loads:
        cp.start()

    barrier = pltpu.get_barrier_semaphore()

    def greet(to):
        pl.semaphore_signal(barrier, inc=1, device_id=to, device_id_type=MESH)

    for d in range(1, NS):
        greet(dev(mod(v + d, NS), y, z))
        greet(dev(v, y, mod(z + d, NZ)))
    for d in range(1, NY):
        greet(dev(v, mod(y + d, NY), z))
    home_diag = v == z
    c_to = mem // 4
    c_row = lax.rem(mem, 4)
    for j in range(4):
        src_mem = 4 * v + j
        is_self = jnp.logical_and(home_diag, src_mem == mem)

        @pl.when(jnp.logical_not(is_self))
        def _():
            greet((z, src_mem))

    for s in range(NS):
        is_self = jnp.logical_and(home_diag, v == s)

        @pl.when(jnp.logical_not(is_self))
        def _():
            greet(dev(s, y, v))

    c_self = jnp.logical_and(home_diag, c_to == v)

    loads[0].wait()

    def cast_one(i, carry):
        xx, g = i // NZ, lax.rem(i, NZ)
        col = pl.multiple_of(g * (NS * data) + (NC * xx + oc) * data, data)
        core_send[xx, g] = par_v[:, pl.ds(col, data)].astype(BF16)
        return carry

    lax.fori_loop(0, NX * NZ, cast_one, 0)
    loads[1].wait()
    loads[2].wait()
    for s in range(NS):
        a0[s] = (per_v[:, s * data:(s + 1) * data] + obs_v[:, s * data:(s + 1) * data]).astype(BF16)

    pl.semaphore_wait(
        barrier,
        (NS - 1) + (NZ - 1) + (NY - 1)
        + 4 - c_self.astype(jnp.int32)
        + NZ - home_diag.astype(jnp.int32),
    )

    sends = []

    def start(cp):
        cp.start()
        sends.append(cp)

    partner = dev(NC * x + oc, y, z)
    for e in (1, 3, 2, 0):
        xx = mod(x + e, NX)
        start(rc(core_send.at[xx], core_recv.at[xx], co_ss.at[e], co_rs.at[xx], partner))

    own_x = pltpu.make_async_copy(ens.at[:, pl.ds(pl.multiple_of(v * cells, cells), cells)], x1.at[v], x1_rs.at[v])
    own_x.start()
    own_a = pltpu.make_async_copy(a0.at[v], a1.at[v], a1_rs.at[v])
    own_a.start()
    for d in range(1, NS):
        to = mod(v + d, NS)
        start(rc(a0.at[to], a1.at[v], a1_ss.at[d], a1_rs.at[v], dev(to, y, z)))
        start(rc(ens.at[:, pl.ds(pl.multiple_of(to * cells, cells), cells)], x1.at[v], x1_ss.at[d], x1_rs.at[v], dev(to, y, z)))

    @pl.when(home_diag)
    def _():
        pltpu.make_async_copy(var.at[v], vh, v_rs).start()
        for d in range(1, NS):
            to = mod(v + d, NS)
            rc(var.at[to], vh, v_ss.at[d], v_rs, dev(to, y, z)).start()

    for yy in range(NY):
        is_self = jnp.logical_and(c_self, y == yy)

        @pl.when(is_self)
        def _():
            pltpu.make_async_copy(coef, ch.at[c_row], c_rs.at[c_row]).start()

        @pl.when(jnp.logical_not(is_self))
        def _():
            rc(coef, ch.at[c_row], c_ss.at[yy], c_rs.at[c_row], dev(c_to, yy, v)).start()

    for e in (1, 3, 2, 0):
        xx = mod(x + e, NX)
        rc(core_send.at[xx], core_recv.at[xx], co_ss.at[e], co_rs.at[xx], partner).wait_recv()

        def sum_one(g, carry):
            col = pl.multiple_of(g * (NS * data) + (NC * xx + c) * data, data)
            total = par_v[:, pl.ds(col, data)] + core_recv[xx, g].astype(F32)
            if e == 0:
                own_sum[g] = total
            else:
                rs_send[e - 1, g] = total.astype(BF16)
            return carry

        lax.fori_loop(0, NZ, sum_one, 0)
        if e:
            start(rc(rs_send.at[e - 1], rs_recv.at[e - 1], rs_ss.at[e - 1], rs_rs.at[e - 1], dev(NC * xx + c, y, z)))

    for d in range(NZ):
        g = mod(z + d, NZ)
        pltpu.make_async_copy(x1.at[g], x1.at[g], x1_rs.at[g]).wait()
        pltpu.make_async_copy(a1.at[g], a1.at[g], a1_rs.at[g]).wait()
        if d == 0:
            pltpu.make_async_copy(x1.at[g], x_all.at[y, z], xz_rs.at[z]).start()
            pltpu.make_async_copy(a1.at[g], a2.at[z], az_rs.at[z]).start()
        else:
            start(rc(a1.at[g], a2.at[z], az_ss.at[d], az_rs.at[z], dev(v, y, g)))
            start(rc(x1.at[g], x_all.at[y, z], xz_ss.at[d], xz_rs.at[z], dev(v, y, g)))

    for e in range(1, NX):
        rc(rs_send.at[e - 1], rs_recv.at[e - 1], rs_ss.at[e - 1], rs_rs.at[e - 1], partner).wait_recv()

    def pred_one(g, carry):
        total = own_sum[g]
        for e in range(NX - 1):
            total += rs_recv[e, g].astype(F32)
        p1[g] = total.astype(BF16)
        return carry

    lax.fori_loop(0, NZ, pred_one, 0)
    pltpu.make_async_copy(p1.at[z], p_all.at[y, z], pz_rs.at[z]).start()
    for d in range(1, NZ):
        g = mod(z + d, NZ)
        start(rc(p1.at[g], p_all.at[y, z], pz_ss.at[d], pz_rs.at[z], dev(v, y, g)))

    def spread_x(e):
        zs = mod(z + NZ - e, NZ)
        pltpu.make_async_copy(x_all.at[y, zs], x_all.at[y, zs], xz_rs.at[zs]).wait()
        for d in range(1, NY):
            start(rc(x_all.at[y, zs], x_all.at[y, zs], xy_ss.at[d, e], xy_rs.at[y, zs], dev(v, mod(y + d, NY), z)))

    for e in range(4):
        spread_x(e)

    for e in range(NZ):
        zs = mod(z + NZ - e, NZ)
        pltpu.make_async_copy(p_all.at[y, zs], p_all.at[y, zs], pz_rs.at[zs]).wait()
    for d in range(1, NY):
        start(rc(p_all.at[y], p_all.at[y], py_ss.at[d], py_rs.at[y], dev(v, mod(y + d, NY), z)))

    for e in range(4, NZ):
        spread_x(e)

    for e in range(NZ):
        zs = mod(z + NZ - e, NZ)
        pltpu.make_async_copy(a2.at[zs], a2.at[zs], az_rs.at[zs]).wait()
    pltpu.make_async_copy(var.at[0], vh, v_rs).wait()

    def weight_one(o, carry):
        col = pl.ds(pl.multiple_of(o * BLK, BLK), BLK)
        innov = a2[:, :, col].astype(F32) - p_all[y, :, :, col].astype(F32)
        w = innov.reshape(nl, BLK) / vh[pl.ds(o, 1), :]
        wt[o] = w.astype(BF16)
        return carry

    lax.fori_loop(0, nob, weight_one, 0)

    for d in range(1, NY):
        ys = mod(y + d, NY)
        pltpu.make_async_copy(p_all.at[ys], p_all.at[ys], py_rs.at[ys]).wait()

    def moment_one(o, carry):
        col = pl.ds(pl.multiple_of(o * BLK, BLK), BLK)
        pred = p_all[:, :, :, col].astype(F32).reshape(NY * nl, BLK)
        anom = (pred - jnp.mean(pred, axis=0, keepdims=True)).astype(BF16)
        mom = lax.dot_general(wt[o], anom, (((1,), (1,)), ((), ())), preferred_element_type=F32)
        for h in range(2):
            m_f[h, pl.ds(o, nl, stride=nob), :] = mom[:, h * 128:(h + 1) * 128]
        return carry

    lax.fori_loop(0, nob, moment_one, 0)

    half = nl // 2
    for q in range(2):
        def cast_m(i, carry):
            rows = pl.ds(pl.multiple_of((q * half + i) * nob, nob), nob)
            for h in range(2):
                m_all[q, v, i, :, h * 128:(h + 1) * 128] = m_f[h, rows, :].astype(BF16)
            return carry

        lax.fori_loop(0, half, cast_m, 0)
        for e in range(1, NX):
            start(rc(m_all.at[q, v], m_all.at[q, v], mx_ss.at[q, e], mx_rs.at[q, v], dev(mod(v + NC * e, NS), y, z)))
        start(rc(m_all.at[q, v], m_all.at[q, v], mc_ss.at[q, 0], mc_rs.at[q, v], partner))

    for j in range(4):
        pltpu.make_async_copy(ch.at[j], ch.at[j], c_rs.at[j]).wait()
    coeff = ch[...].reshape(nvb, BLK)

    for q in range(2):
        for e in (1, 3, 2):
            vs = mod(v + NC * e, NS)
            pltpu.make_async_copy(m_all.at[q, vs], m_all.at[q, vs], mx_rs.at[q, vs]).wait()
            start(rc(m_all.at[q, vs], m_all.at[q, vs], mc_ss.at[q, e], mc_rs.at[q, vs], partner))
        for e in range(NX):
            vs = NC * mod(x + e, NX) + oc
            pltpu.make_async_copy(m_all.at[q, vs], m_all.at[q, vs], mc_rs.at[q, vs]).wait()

        def combine_one(i, carry):
            mom = m_all[q, :, i].reshape(NS * nob, NY * nl)
            com = jnp.dot(coeff, mom, preferred_element_type=F32)
            for h in range(2):
                comb[h, pl.ds(q * half + i, nvb, stride=nl), :] = com[:, h * 128:(h + 1) * 128]
            return carry

        lax.fori_loop(0, half, combine_one, 0)

    for d in range(1, NY):
        ys = mod(y + d, NY)
        for e in range(NZ):
            pltpu.make_async_copy(x_all.at[ys, e], x_all.at[ys, e], xy_rs.at[ys, e]).wait()

    parts = 4
    per_part = nvb // parts
    width = per_part * BLK
    for q in range(parts):
        def update_one(i, carry):
            b = q * per_part + i
            col = pl.ds(pl.multiple_of(b * BLK, BLK), BLK)
            state = x_all[:, :, :, col].astype(F32).reshape(NY * nl, BLK)
            anom = (state - jnp.mean(state, axis=0, keepdims=True)).astype(BF16)
            rows = pl.ds(pl.multiple_of(b * nl, nl), nl)
            inc = jnp.zeros((nl, BLK), F32)
            for h in range(2):
                inc += jnp.dot(
                    comb[h, rows, :].astype(BF16), anom[h * 128:(h + 1) * 128], preferred_element_type=F32
                )
            own = x_all[y, :, :, col].astype(F32)
            ost[:, :, col] = (own + inc.reshape(NZ, MEM, BLK) * (1.0 / (NY * nl - 1))).astype(BF16)
            return carry

        lax.fori_loop(0, per_part, update_one, 0)
        src_col = pl.ds(q * width, width)
        dst_col = pl.ds(pl.multiple_of(v * cells + q * width, width), width)
        for d in range(NZ):
            zt = mod(z + d, NZ)
            if d == 0:
                @pl.when(home_diag)
                def _():
                    pltpu.make_async_copy(ost.at[zt, :, src_col], out.at[:, dst_col], o_rs.at[q, v]).start()

                @pl.when(jnp.logical_not(home_diag))
                def _():
                    rc(ost.at[zt, :, src_col], out.at[:, dst_col], o_ss.at[q, 0], o_rs.at[q, v], dev(z, y, zt)).start()
            else:
                start(rc(ost.at[zt, :, src_col], out.at[:, dst_col], o_ss.at[q, d], o_rs.at[q, v], dev(z, y, zt)))

    for cp in sends:
        cp.wait_send()

    @pl.when(home_diag)
    def _():
        for d in range(1, NS):
            rc(var.at[0], vh, v_ss.at[d], v_rs, partner).wait_send()

    for yy in range(NY):
        @pl.when(jnp.logical_not(jnp.logical_and(c_self, y == yy)))
        def _():
            rc(coef, ch.at[c_row], c_ss.at[yy], c_rs.at[c_row], partner).wait_send()

    @pl.when(jnp.logical_not(home_diag))
    def _():
        for q in range(parts):
            rc(ost.at[0, :, pl.ds(0, width)], out.at[:, pl.ds(0, width)], o_ss.at[q, 0], o_rs.at[q, v], partner).wait_send()

    for q in range(parts):
        for s in range(NS):
            dst_col = pl.ds(s * cells + q * width, width)
            pltpu.make_async_copy(out.at[:, dst_col], out.at[:, dst_col], o_rs.at[q, s]).wait()


def local(ensemble, partials, perturb, observed, variance, obs_lists, taper_index, taper_table):
    groups = observed.shape[0] // BLK
    table_hits = (
        taper_index[:, :, None] == jnp.arange(taper_table.shape[0], dtype=jnp.int32)[None, None, :]
    ).astype(F32)
    tapers = jnp.sum(table_hits * taper_table[None, None, :], axis=2)
    picks = (obs_lists[:, :, None] == jnp.arange(groups, dtype=jnp.int32)[None, None, :]).astype(F32)
    coeff = jnp.sum(tapers[:, :, None] * picks, axis=1).astype(BF16)
    cells = ensemble.shape[1] // NS
    data = perturb.shape[1] // NS
    nob = data // BLK
    nl = NZ * MEM
    nvb = cells // BLK
    dma = pltpu.SemaphoreType.DMA
    return pl.pallas_call(
        kernel,
        out_shape=jax.ShapeDtypeStruct(ensemble.shape, BF16),
        in_specs=[pl.BlockSpec(memory_space=pl.ANY)] * 6,
        out_specs=pl.BlockSpec(memory_space=pl.ANY),
        scratch_shapes=[
            pltpu.VMEM(partials.shape[1:], F32),
            pltpu.VMEM(perturb.shape, F32),
            pltpu.VMEM((1, observed.shape[0]), F32),
            pltpu.VMEM((NX, NZ, MEM, data), BF16),
            pltpu.VMEM((NX, NZ, MEM, data), BF16),
            pltpu.VMEM((NX - 1, NZ, MEM, data), BF16),
            pltpu.VMEM((NX - 1, NZ, MEM, data), BF16),
            pltpu.VMEM((NZ, MEM, data), F32),
            pltpu.VMEM((NS, MEM, data), BF16),
            pltpu.VMEM((NS, MEM, data), BF16),
            pltpu.VMEM((NZ, MEM, data), BF16),
            pltpu.VMEM((nob, BLK), F32),
            pltpu.VMEM((4, 16, BLK), BF16),
            pltpu.VMEM((NZ, MEM, data), BF16),
            pltpu.VMEM((NY, NZ, MEM, data), BF16),
            pltpu.VMEM((NS, MEM, cells), BF16),
            pltpu.VMEM((NY, NZ, MEM, cells), BF16),
            pltpu.VMEM((nob, nl, BLK), BF16),
            pltpu.VMEM((2, nl * nob, 128), F32),
            pltpu.VMEM((2, NS, nl // 2, nob, NY * nl), BF16),
            pltpu.VMEM((2, nvb * nl, 128), F32),
            pltpu.VMEM((NZ, MEM, cells), BF16),
            dma((3,)), dma((1,)),
            dma((NX,)), dma((NX,)),
            dma((NX - 1,)), dma((NX - 1,)),
            dma((NS,)), dma((NS,)),
            dma((NS,)), dma((NS,)),
            dma((NS,)), dma(()),
            dma((NY,)), dma((4,)),
            dma((NZ,)), dma((NZ,)),
            dma((NZ,)), dma((NZ,)),
            dma((NZ,)), dma((NZ,)),
            dma((NY,)), dma((NY,)),
            dma((NY, NZ)), dma((NY, NZ)),
            dma((2, NX)), dma((2, NS)),
            dma((2, NX)), dma((2, NS)),
            dma((4, NZ)), dma((4, NS)),
        ],
        compiler_params=pltpu.CompilerParams(
            collective_id=0, has_side_effects=True, vmem_limit_bytes=56 * 1024 * 1024
        ),
        cost_estimate=pl.CostEstimate(flops=900_000_000, bytes_accessed=8_000_000, transcendentals=0),
        name="update",
    )(
        ensemble,
        partials,
        perturb,
        observed.reshape(1, -1),
        variance.reshape(NS, nob, BLK),
        coeff,
    )


def solution(mesh):
    return jax.shard_map(
        local,
        mesh=mesh,
        in_specs=(
            P("mem", "vox"),
            P("vox", "mem", None),
            P("mem", "vox"),
            P("vox"),
            P("vox"),
            P(("vox", "mem"), None),
            P(("vox", "mem"), None),
            P(),
        ),
        out_specs=P("mem", "vox"),
        check_vma=False,
    )
```

time: 377 us -> 150 us (0.40)
  waiting for transfers between devices: 228 us -> 0 us
  Pallas kernels: 0 us -> 143 us
  matrix products: 63 us -> 0 us
  blocking collectives: 30 us -> 0 us
  local copies, waits for them, and re-layouts: 17.6 us -> 2.26 us
  between operations: 13.3 us -> 0.01 us
  starting transfers between devices: 9.41 us -> 0 us
  other arithmetic: 11.6 us -> 2.46 us
    all_gather x2 -> x0, waiting for transfers between devices: 166 us -> none  [the longest x1 93.4 us: local(): lax.all_gather(weights, 'mem', axis=0, tiled=True)]
    pallas_call x0 -> x1, Pallas kernels: none -> 143 us  [local(): pl.pallas_call(kernel, out_shape=jax.ShapeDtypeStruct(ensemble.shape, BF1...]
    dot_general x3 -> x0, matrix products: 63 us -> none  [the longest x1 43.5 us: from_moments(): jnp.einsum('bo,okl->bkl', coeff, moments, precision=high)]
    reduce_scatter x1 -> x0, waiting for transfers between devices: 37.5 us -> none  [local(): lax.psum_scatter(partials[0].astype(jnp.bfloat16), 'vox', scatter_dimensi...]
    all_to_all x1 -> x0, blocking collectives: 30 us -> none  [local(): lax.all_to_all(updated, 'mem', split_axis=0, concat_axis=1, tiled=True)]
    all_to_all x1 -> x0, waiting for transfers between devices: 24.6 us -> none  [local(): lax.all_to_all(ensemble, 'mem', split_axis=1, concat_axis=0, tiled=True)]
    all_gather x1 -> x0, local copies, waits for them, and re-layouts: 11.9 us -> none  [local(): lax.all_gather(weights, 'mem', axis=0, tiled=True)]
    all_to_all x1 -> x0, starting transfers between devices: 9.33 us -> none  [local(): lax.all_to_all(ensemble, 'mem', split_axis=1, concat_axis=0, tiled=True)]
  transfers between devices with their start and end apart: 4 -> 0, of which waited for: 4 -> 0; matrix products, arithmetic and copies ran while one was open for 2% -> 0% of each run, Pallas kernels for 0% -> 0%
where the time goes in v1:
time: 150 us; the launch traced here: 147 us
  Pallas kernels  143 us (95%)
  other arithmetic  2.46 us (2%)
  local copies, waits for them, and re-layouts  2.26 us (2%)
    pallas_call x1, Pallas kernels, local(): pl.pallas_call(kernel, out_shape=jax.ShapeDtypeStruct(ensemble.shape, BF1...  143 us

profile of v1, /device:TPU:1, one launch (start us, length us, event | category | flops | bytes accessed | tf_op | source)
XLA Modules:
  0.0 147.3 jit_solution(12910596007399718941)
XLA Ops:
  0.0 0.8 select_reduce_fusion.1
  0.8 1.6 %select_reduce_fusion.coef = bf16[16,128]{1,0:T(8,128)(2,1)} fusion(f32[16,64]{1,0:T(8,128)S(1)} %select_reduce_fusion.1, s32[16,64]{1,0:T(8,128)} %param.13), kind=kLoop, calls=%fused_computation | loop fusion | flops 391168 | bytes 12288 | tf_op jit(solution)/shard_map/reduce_sum | solution.py:343
  2.5 142.6 %update.1 = bf16[8,65536]{1,0:T(8,128)(2,1)} custom-call(bf16[8,65536]{1,0:T(8,128)(2,1)} %ens.1, f32[1,8,131072]{2,1,0:T(8,128)} %par.1, f32[8,16384]{1,0:T(8,128)} %per.1, f32[1,16384]{1,0:T(1,128)} %bitcast.2, f32[8,16,128]{2,1,0:T(8,128)} %bitcast.3, bf16[16,128]{1,0:T(8,128)(2,1)} %select_reduce_fusion.coef), custom_call_target="tpu_custom_call" | custom-call | flops 900000000 | bytes 8000000 | tf_op jit(solution)/shard_map/update/pallas_call | solution.py:350
  145.1 2.3 %copy.10 = bf16[8,65536]{1,0:T(8,128)(2,1)} copy(bf16[8,65536]{1,0:T(8,128)(2,1)} %update.1) | data formatting | bytes 2097152

commit v2 on v1

v2 whole, which is shorter than its diff:
```python
import functools

import jax
import jax.numpy as jnp
from jax import lax
from jax.experimental import pallas as pl
from jax.experimental.pallas import tpu as pltpu
from jax.sharding import PartitionSpec as P

MESH = pl.DeviceIdType.MESH
NX, NC, NY, NZ = 4, 2, 4, 8
NS = NX * NC
MEM = 8
BLK = 128
F32, BF16 = jnp.float32, jnp.bfloat16
X1_EARLY = ()


def loop(n, fn):
    lax.fori_loop(0, n, fn, 0)


def kernel(
    ens, par, per, obs, var, lists, tap_i, tap_t, out,
    par_v, per_v, obs_v, lists_v, tap_iv, tap_tv, core_send, core_recv, rs_send, rs_recv, own_sum,
    a0, a1, a2, vh, c0, ch, p1, p_all, x1, x_all, xc, wt, m_f, m_all, comb, ost,
    ld_s,
    co_ss, co_rs, rs_ss, rs_rs, x1_ss, x1_rs, a1_ss, a1_rs, v_ss, v_rs, c_ss, c_rs,
    xz_ss, xz_rs, az_ss, az_rs, pz_ss, pz_rs, py_ss, py_rs, xy_ss, xy_rs, xr_ss, xr_rs,
    mx_ss, mx_rs, mr_ss, mr_rs, mc_ss, mc_rs, o_ss, o_rs,
):
    v = lax.axis_index("vox")
    mem = lax.axis_index("mem")
    x, c = v // NC, lax.rem(v, NC)
    y, z = mem // NZ, lax.rem(mem, NZ)
    oc = 1 - c
    cells = ens.shape[1] // NS
    data = per.shape[1] // NS
    hdata = data // 2
    nob = data // BLK // 2
    nvb = cells // BLK
    nl = NZ * MEM
    nk = NY * nl
    hc = cells // 2

    def dev(vox, yy, zz):
        return (vox, yy * NZ + zz)

    def rc(src, dst, ss, rs, to):
        return pltpu.make_async_remote_copy(
            src_ref=src, dst_ref=dst, send_sem=ss, recv_sem=rs, device_id=to, device_id_type=MESH
        )

    def arrived(ref, sem):
        pltpu.make_async_copy(ref, ref, sem).wait()

    def mod(a, n):
        return lax.rem(a, n)

    partner = dev(NC * x + oc, y, z)

    loads = [
        pltpu.make_async_copy(src, dst, ld_s.at[i])
        for i, (src, dst) in enumerate(
            [(par.at[0], par_v), (per, per_v), (obs, obs_v), (lists, lists_v), (tap_i, tap_iv), (tap_t, tap_tv)]
        )
    ]
    for cp in loads:
        cp.start()

    barrier = pltpu.get_barrier_semaphore()

    def greet(to):
        pl.semaphore_signal(barrier, inc=1, device_id=to, device_id_type=MESH)

    for d in range(1, NS):
        greet(dev(mod(v + d, NS), y, z))
        greet(dev(v, y, mod(z + d, NZ)))
    for d in range(1, NY):
        greet(dev(v, mod(y + d, NY), z))
    home_diag = v == z
    c_to = mem // 4
    c_row = lax.rem(mem, 4)
    for j in range(4):
        src_mem = 4 * v + j
        is_self = jnp.logical_and(home_diag, src_mem == mem)

        @pl.when(jnp.logical_not(is_self))
        def _():
            greet((z, src_mem))

    for s in range(NS):
        is_self = jnp.logical_and(home_diag, v == s)

        @pl.when(jnp.logical_not(is_self))
        def _():
            greet(dev(s, y, v))

    c_self = jnp.logical_and(home_diag, c_to == v)

    loads[0].wait()

    def cast_one(i, carry):
        xx, g = i // NZ, lax.rem(i, NZ)
        for q in range(2):
            col = pl.multiple_of(g * (NS * data) + (NC * xx + oc) * data + q * hdata, hdata)
            core_send[q, xx, g] = par_v[:, pl.ds(col, hdata)].astype(BF16)
        return carry

    loop(NX * NZ, cast_one)
    for cp in loads[1:]:
        cp.wait()
    for s in range(NS):
        a0[s] = (per_v[:, s * data:(s + 1) * data] + obs_v[:, s * data:(s + 1) * data]).astype(BF16)
    tapers = jnp.zeros(tap_iv.shape, F32)
    for t in range(tap_tv.shape[1]):
        tapers += jnp.where(tap_iv[...] == t, tap_tv[:, t:t + 1], 0.0)
    lanes = lax.broadcasted_iota(jnp.int32, (tap_iv.shape[0], BLK), 1)
    coeff = jnp.zeros((tap_iv.shape[0], BLK), F32)
    for j in range(tap_iv.shape[1]):
        coeff += jnp.where(lists_v[:, j:j + 1] == lanes, tapers[:, j:j + 1], 0.0)
    c0[...] = coeff.astype(BF16)

    pl.semaphore_wait(
        barrier,
        (NS - 1) + (NZ - 1) + (NY - 1)
        + 4 - c_self.astype(jnp.int32)
        + NZ - home_diag.astype(jnp.int32),
    )

    sends = []

    def start(cp):
        cp.start()
        sends.append(cp)

    def core_copy(q, e):
        xx = mod(x + e, NX)
        return rc(core_send.at[q, xx], core_recv.at[q, xx], co_ss.at[q, e], co_rs.at[q, xx], partner)

    for q in range(2):
        for e in (2, 1, 3, 0):
            start(core_copy(q, e))

    pltpu.make_async_copy(a0.at[v], a1.at[v], a1_rs.at[v]).start()
    pltpu.make_async_copy(ens.at[:, pl.ds(pl.multiple_of(v * cells, cells), cells)], x1.at[v], x1_rs.at[v]).start()
    for d in range(1, NS):
        to = mod(v + d, NS)
        start(rc(a0.at[to], a1.at[v], a1_ss.at[d], a1_rs.at[v], dev(to, y, z)))

    def send_x1(d):
        to = mod(v + d, NS)
        start(rc(ens.at[:, pl.ds(pl.multiple_of(to * cells, cells), cells)], x1.at[v], x1_ss.at[d], x1_rs.at[v], dev(to, y, z)))

    for d in X1_EARLY:
        send_x1(d)

    @pl.when(home_diag)
    def _():
        pltpu.make_async_copy(var.at[v], vh, v_rs).start()
        for d in range(1, NS):
            to = mod(v + d, NS)
            rc(var.at[to], vh, v_ss.at[d], v_rs, dev(to, y, z)).start()

    for yy in range(NY):
        is_self = jnp.logical_and(c_self, y == yy)

        @pl.when(is_self)
        def _():
            pltpu.make_async_copy(c0, ch.at[c_row], c_rs.at[c_row]).start()

        @pl.when(jnp.logical_not(is_self))
        def _():
            rc(c0, ch.at[c_row], c_ss.at[yy], c_rs.at[c_row], dev(c_to, yy, v)).start()

    for q in range(2):
        for e in (2, 1, 3, 0):
            xx = mod(x + e, NX)
            core_copy(q, e).wait_recv()

            def sum_one(g, carry):
                col = pl.multiple_of(g * (NS * data) + (NC * xx + c) * data + q * hdata, hdata)
                total = par_v[:, pl.ds(col, hdata)] + core_recv[q, xx, g].astype(F32)
                if e == 0:
                    own_sum[q, g] = total
                else:
                    rs_send[q, e - 1, g] = total.astype(BF16)
                return carry

            loop(NZ, sum_one)
            if e:
                start(rc(rs_send.at[q, e - 1], rs_recv.at[q, e - 1], rs_ss.at[q, e - 1], rs_rs.at[q, e - 1], dev(NC * xx + c, y, z)))

    for d in range(1, NS):
        if d not in X1_EARLY:
            send_x1(d)

    def forward_a(d):
        g = mod(z + d, NZ)
        arrived(a1.at[g], a1_rs.at[g])
        if d == 0:
            pltpu.make_async_copy(a1.at[g], a2.at[z], az_rs.at[z]).start()
        else:
            start(rc(a1.at[g], a2.at[z], az_ss.at[d], az_rs.at[z], dev(v, y, g)))

    def forward_x(d):
        g = mod(z + d, NZ)
        arrived(x1.at[g], x1_rs.at[g])
        if d == 0:
            pltpu.make_async_copy(x1.at[g], x_all.at[y, z], xz_rs.at[z]).start()
        else:
            start(rc(x1.at[g], x_all.at[y, z], xz_ss.at[d], xz_rs.at[z], dev(v, y, g)))

    def predict(q):
        for e in range(1, NX):
            rc(rs_send.at[q, e - 1], rs_recv.at[q, e - 1], rs_ss.at[q, e - 1], rs_rs.at[q, e - 1], partner).wait_recv()

        def pred_one(g, carry):
            total = own_sum[q, g]
            for e in range(NX - 1):
                total += rs_recv[q, e, g].astype(F32)
            p1[q, g] = total.astype(BF16)
            return carry

        loop(NZ, pred_one)
        pltpu.make_async_copy(p1.at[q, z], p_all.at[q, y, z], pz_rs.at[q, z]).start()
        for d in range(1, NZ):
            g = mod(z + d, NZ)
            start(rc(p1.at[q, g], p_all.at[q, y, z], pz_ss.at[q, d], pz_rs.at[q, z], dev(v, y, g)))

    def spread_p(q):
        for e in range(NZ):
            zs = mod(z + NZ - e, NZ)
            arrived(p_all.at[q, y, zs], pz_rs.at[q, zs])
        for d in (2, 1, 3):
            start(rc(p_all.at[q, y], p_all.at[q, y], py_ss.at[q, d], py_rs.at[q, y], dev(v, mod(y + d, NY), z)))

    ylo, yhi = mod(y + NY - 1, NY), mod(y + 1, NY)

    def spread_x(e):
        zs = mod(z + NZ - e, NZ)
        arrived(x_all.at[y, zs], xz_rs.at[zs])
        for i, yy in enumerate((yhi, ylo)):
            start(rc(x_all.at[y, zs], x_all.at[y, zs], xy_ss.at[i, e], xy_rs.at[y, zs], dev(v, yy, z)))

    def relay_x(e):
        zs = mod(z + NZ - e, NZ)
        for i, (src, to) in enumerate(((ylo, yhi), (yhi, ylo))):
            arrived(x_all.at[src, zs], xy_rs.at[src, zs])
            part = x_all.at[src, zs, :, pl.ds(i * hc, hc)]
            start(rc(part, part, xr_ss.at[i, e], xr_rs.at[i, zs], dev(v, to, z)))

    def settle_x(e):
        zs = mod(z + NZ - e, NZ)
        yo = mod(y + 2, NY)
        for i in range(2):
            arrived(x_all.at[yo, zs, :, pl.ds(i * hc, hc)], xr_rs.at[i, zs])

    def settle_a():
        for e in range(NZ):
            zs = mod(z + NZ - e, NZ)
            arrived(a2.at[zs], az_rs.at[zs])
        arrived(vh, v_rs)

    def weigh(q):
        def weight_one(o, carry):
            col = pl.ds(pl.multiple_of(o * BLK, BLK), BLK)
            acol = pl.ds(pl.multiple_of(q * hdata + o * BLK, BLK), BLK)
            innov = a2[:, :, acol].astype(F32) - p_all[q, y, :, :, col].astype(F32)
            w = innov.reshape(nl, BLK) / vh[pl.ds(q * nob + o, 1), :]
            wt[q * nob + o] = w.astype(BF16)
            return carry

        loop(nob, weight_one)

    hl = nl // 4

    def moments(q):
        for d in range(1, NY):
            ys = mod(y + d, NY)
            arrived(p_all.at[q, ys], py_rs.at[q, ys])

        def moment_one(o, carry):
            col = pl.ds(pl.multiple_of(o * BLK, BLK), BLK)
            pred = p_all[q, :, :, :, col].astype(F32).reshape(nk, BLK).astype(BF16)
            mom = lax.dot_general(wt[q * nob + o], pred, (((1,), (1,)), ((), ())), preferred_element_type=F32)
            mom = mom - jnp.mean(mom, axis=1, keepdims=True)
            for h in range(2):
                m_f[h, pl.ds(o, nl, stride=nob), :] = mom[:, h * 128:(h + 1) * 128]
            return carry

        loop(nob, moment_one)
        for k in range(2):
            def cast_m(i, carry):
                rows = pl.ds(pl.multiple_of((k * hl + i) * 2 * nob, 2 * nob), 2 * nob)
                for h in range(2):
                    m_all[q, k, v, i, :, h * 128:(h + 1) * 128] = m_f[h, rows, :].astype(BF16)
                return carry

            loop(hl, cast_m)
            mine = m_all.at[q, k, v]
            for i, e in enumerate((1, 3)):
                start(rc(mine, mine, mx_ss.at[q, k, i], mx_rs.at[q, k, v], dev(mod(v + NC * e, NS), y, z)))
            start(rc(mine, mine, mc_ss.at[q, k, 0], mc_rs.at[q, k, v], partner))

    def relay_m(q, k):
        lo, hi = mod(v + NC * 3, NS), mod(v + NC, NS)
        for i, (src, to) in enumerate(((lo, hi), (hi, lo))):
            arrived(m_all.at[q, k, src], mx_rs.at[q, k, src])
            part = m_all.at[q, k, src, pl.ds(i * (hl // 2), hl // 2)]
            start(rc(part, part, mr_ss.at[q, k, i], mr_rs.at[q, k, i], dev(to, y, z)))
            whole = m_all.at[q, k, src]
            start(rc(whole, whole, mc_ss.at[q, k, 1 + i], mc_rs.at[q, k, src], partner))

    def finish_m(q, k):
        far = mod(v + NC * 2, NS)
        for i in range(2):
            arrived(m_all.at[q, k, far, pl.ds(i * (hl // 2), hl // 2)], mr_rs.at[q, k, i])
        whole = m_all.at[q, k, far]
        start(rc(whole, whole, mc_ss.at[q, k, 3], mc_rs.at[q, k, far], partner))

    def settle_m(q, k):
        for e in range(NX):
            vs = NC * mod(x + e, NX) + oc
            arrived(m_all.at[q, k, vs], mc_rs.at[q, k, vs])

    def spread_coeff():
        for j in range(4):
            arrived(ch.at[j], c_rs.at[j])
        rows = lax.broadcasted_iota(jnp.int32, (BLK, 2 * BLK), 0)
        cols = lax.broadcasted_iota(jnp.int32, (BLK, 2 * BLK), 1)
        block = lax.rem(cols // (2 * nob), NS) * (2 * nob) + (cols // BLK) * nob + lax.rem(cols, nob)
        tap = ch[...].reshape(nvb, BLK)
        res = []
        for parity in range(2):
            pick = jnp.logical_and(rows == block, lax.rem(cols // nob, 2) == parity)
            res.append(jnp.dot(tap, jnp.where(pick, 1.0, 0.0).astype(BF16), preferred_element_type=F32))
        return jnp.concatenate(res, axis=0).astype(BF16)

    def combine(coeff, k):
        def combine_one(i, carry):
            mom = m_all[:, k, :, i].reshape(2 * NS * 2 * nob, nk)
            com = jnp.dot(coeff, mom, preferred_element_type=F32)
            for parity in range(2):
                rows = pl.ds((k * hl + i) * 2 + parity, nvb, stride=nl)
                for h in range(2):
                    comb[h, rows, :] = com[parity * nvb:(parity + 1) * nvb, h * 128:(h + 1) * 128]
            return carry

        loop(hl, combine_one)

    def centre():
        def centre_one(b, carry):
            col = pl.ds(pl.multiple_of(b * BLK, BLK), BLK)
            state = x_all[:, :, :, col].astype(F32).reshape(nk, BLK)
            xc[b] = (state - jnp.mean(state, axis=0, keepdims=True)).astype(BF16)
            return carry

        loop(nvb, centre_one)

    parts = 4
    per_part = nvb // parts
    width = per_part * BLK

    def update(q):
        def update_one(i, carry):
            b = q * per_part + i
            col = pl.ds(pl.multiple_of(b * BLK, BLK), BLK)
            rows = pl.ds(pl.multiple_of(b * nl, nl), nl)
            left = jnp.concatenate([comb[h, rows, :].astype(BF16) for h in range(2)], axis=1)
            inc = jnp.dot(left, xc[b], preferred_element_type=F32)
            own = x_all[y, :, :, col].astype(F32)
            ost[:, :, col] = (own + inc.reshape(NZ, MEM, BLK) * (1.0 / (nk - 1))).astype(BF16)
            return carry

        loop(per_part, update_one)
        src_col = pl.ds(q * width, width)
        dst_col = pl.ds(pl.multiple_of(v * cells + q * width, width), width)
        for d in range(NZ):
            zt = mod(z + d, NZ)
            src, dst = ost.at[zt, :, src_col], out.at[:, dst_col]
            if d == 0:
                @pl.when(home_diag)
                def _():
                    pltpu.make_async_copy(src, dst, o_rs.at[q, v]).start()

                @pl.when(jnp.logical_not(home_diag))
                def _():
                    rc(src, dst, o_ss.at[q, 0], o_rs.at[q, v], dev(z, y, zt)).start()
            else:
                start(rc(src, dst, o_ss.at[q, d], o_rs.at[q, v], dev(z, y, zt)))

    for d in range(NZ):
        forward_a(d)
    predict(0)
    predict(1)
    for d in range(4):
        forward_x(d)
    spread_p(0)
    for d in range(4, NZ):
        forward_x(d)
    spread_p(1)
    settle_a()
    weigh(0)
    weigh(1)
    for e in range(2):
        spread_x(e)
    moments(0)
    for e in range(2, 4):
        spread_x(e)
    moments(1)
    for e in range(4, NZ):
        spread_x(e)
    coeff = spread_coeff()
    for i, (q, k) in enumerate(((0, 0), (0, 1), (1, 0), (1, 1))):
        relay_x(2 * i)
        relay_m(q, k)
        relay_x(2 * i + 1)
        finish_m(q, k)
    settle_m(0, 0)
    settle_m(1, 0)
    combine(coeff, 0)
    settle_m(0, 1)
    settle_m(1, 1)
    combine(coeff, 1)
    for e in range(NZ):
        settle_x(e)
    centre()
    for q in range(parts):
        update(q)

    for cp in sends:
        cp.wait_send()

    @pl.when(home_diag)
    def _():
        for d in range(1, NS):
            rc(var.at[0], vh, v_ss.at[d], v_rs, partner).wait_send()

    for yy in range(NY):
        @pl.when(jnp.logical_not(jnp.logical_and(c_self, y == yy)))
        def _():
            rc(c0, ch.at[c_row], c_ss.at[yy], c_rs.at[c_row], partner).wait_send()

    @pl.when(jnp.logical_not(home_diag))
    def _():
        for q in range(parts):
            rc(ost.at[0, :, pl.ds(0, width)], out.at[:, pl.ds(0, width)], o_ss.at[q, 0], o_rs.at[q, v], partner).wait_send()

    for q in range(parts):
        for s in range(NS):
            dst_col = pl.ds(s * cells + q * width, width)
            arrived(out.at[:, dst_col], o_rs.at[q, s])


def local(ensemble, partials, perturb, observed, variance, obs_lists, taper_index, taper_table):
    cells = ensemble.shape[1] // NS
    data = perturb.shape[1] // NS
    nob = data // BLK
    nl = NZ * MEM
    nvb = cells // BLK
    hdata = data // 2
    dma = pltpu.SemaphoreType.DMA
    return pl.pallas_call(
        kernel,
        out_shape=jax.ShapeDtypeStruct(ensemble.shape, BF16),
        in_specs=[pl.BlockSpec(memory_space=pl.ANY)] * 8,
        out_specs=pl.BlockSpec(memory_space=pl.ANY),
        scratch_shapes=[
            pltpu.VMEM(partials.shape[1:], F32),
            pltpu.VMEM(perturb.shape, F32),
            pltpu.VMEM((1, observed.shape[0]), F32),
            pltpu.VMEM(obs_lists.shape, jnp.int32),
            pltpu.VMEM(taper_index.shape, jnp.int32),
            pltpu.VMEM((1, taper_table.shape[0]), F32),
            pltpu.VMEM((2, NX, NZ, MEM, hdata), BF16),
            pltpu.VMEM((2, NX, NZ, MEM, hdata), BF16),
            pltpu.VMEM((2, NX - 1, NZ, MEM, hdata), BF16),
            pltpu.VMEM((2, NX - 1, NZ, MEM, hdata), BF16),
            pltpu.VMEM((2, NZ, MEM, hdata), F32),
            pltpu.VMEM((NS, MEM, data), BF16),
            pltpu.VMEM((NS, MEM, data), BF16),
            pltpu.VMEM((NZ, MEM, data), BF16),
            pltpu.VMEM((nob, BLK), F32),
            pltpu.VMEM((16, BLK), BF16),
            pltpu.VMEM((4, 16, BLK), BF16),
            pltpu.VMEM((2, NZ, MEM, hdata), BF16),
            pltpu.VMEM((2, NY, NZ, MEM, hdata), BF16),
            pltpu.VMEM((NS, MEM, cells), BF16),
            pltpu.VMEM((NY, NZ, MEM, cells), BF16),
            pltpu.VMEM((nvb, NY * nl, BLK), BF16),
            pltpu.VMEM((nob, nl, BLK), BF16),
            pltpu.VMEM((2, nl * nob // 2, 128), F32),
            pltpu.VMEM((2, 2, NS, nl // 4, nob, NY * nl), BF16),
            pltpu.VMEM((2, nvb * nl, 128), F32),
            pltpu.VMEM((NZ, MEM, cells), BF16),
            dma((6,)),
            dma((2, NX)), dma((2, NX)),
            dma((2, NX - 1)), dma((2, NX - 1)),
            dma((NS,)), dma((NS,)),
            dma((NS,)), dma((NS,)),
            dma((NS,)), dma(()),
            dma((NY,)), dma((4,)),
            dma((NZ,)), dma((NZ,)),
            dma((NZ,)), dma((NZ,)),
            dma((2, NZ)), dma((2, NZ)),
            dma((2, NY)), dma((2, NY)),
            dma((2, NZ)), dma((NY, NZ)),
            dma((2, NZ)), dma((2, NZ)),
            dma((2, 2, 2)), dma((2, 2, NS)),
            dma((2, 2, 2)), dma((2, 2, 2)),
            dma((2, 2, 4)), dma((2, 2, NS)),
            dma((4, NZ)), dma((4, NS)),
        ],
        compiler_params=pltpu.CompilerParams(
            collective_id=0, has_side_effects=True, vmem_limit_bytes=58 * 1024 * 1024
        ),
        cost_estimate=pl.CostEstimate(flops=900_000_000, bytes_accessed=8_000_000, transcendentals=0),
        name="update",
    )(
        ensemble,
        partials,
        perturb,
        observed.reshape(1, -1),
        variance.reshape(NS, nob, BLK),
        obs_lists,
        taper_index,
        taper_table.reshape(1, -1),
    )


def solution(mesh):
    return jax.shard_map(
        local,
        mesh=mesh,
        in_specs=(
            P("mem", "vox"),
            P("vox", "mem", None),
            P("mem", "vox"),
            P("vox"),
            P("vox"),
            P(("vox", "mem"), None),
            P(("vox", "mem"), None),
            P(),
        ),
        out_specs=P("mem", "vox"),
        check_vma=False,
    )
```

time: 150 us -> 126 us (0.84)
  Pallas kernels: 143 us -> 121 us
  other arithmetic: 2.46 us -> 0 us
    pallas_call x1, Pallas kernels: 143 us -> 121 us  [local(): pl.pallas_call(kernel, out_shape=jax.ShapeDtypeStruct(ensemble.shape, BF1...]
    reduce_sum x2 -> x0, other arithmetic: 2.46 us -> none  [the longest x1 1.64 us: local(): coeff = jnp.sum(tapers[:, :, None] * picks, axis=1).astype(BF16)]
where the time goes in v2:
time: 126 us; the launch traced here: 124 us
  Pallas kernels  121 us (96%)
  local copies, waits for them, and re-layouts  2.26 us (2%)
    pallas_call x1, Pallas kernels, local(): pl.pallas_call(kernel, out_shape=jax.ShapeDtypeStruct(ensemble.shape, BF1...  121 us

profile of v2, /device:TPU:1, one launch (start us, length us, event | category | flops | bytes accessed | tf_op | source)
XLA Modules:
  0.0 123.6 jit_solution(10555618868006882472)
XLA Ops:
  0.0 121.3 %update.1 = bf16[8,65536]{1,0:T(8,128)(2,1)} custom-call(bf16[8,65536]{1,0:T(8,128)(2,1)} %ens.1, f32[1,8,131072]{2,1,0:T(8,128)} %par.1, f32[8,16384]{1,0:T(8,128)} %per.1, f32[1,16384]{1,0:T(1,128)} %bitcast.3, f32[8,16,128]{2,1,0:T(8,128)} %bitcast.4, s32[16,64]{1,0:T(8,128)} %lists.1, s32[16,64]{1,0:T(8,128)} %tap_i.1, f32[1,16]{1,0:T(1,128)} %bitcast.5), custom_call_target="tpu_custom_call" | custom-call | flops 900000000 | bytes 8000000 | tf_op jit(solution)/shard_map/update/pallas_call | solution.py:464
  121.3 2.3 %copy.10 = bf16[8,65536]{1,0:T(8,128)(2,1)} copy(bf16[8,65536]{1,0:T(8,128)(2,1)} %update.1) | data formatting | bytes 2097152

commit v3 on v2

--- a/solution.py
+++ b/solution.py
@@ -13,11 +13,18 @@
 MEM = 8
 BLK = 128
 F32, BF16 = jnp.float32, jnp.bfloat16
-X1_EARLY = ()
-
-
-def loop(n, fn):
-    lax.fori_loop(0, n, fn, 0)
+PARTS = 4
+EARLY = 0
+
+
+def loop(n, fn, unroll=1):
+
+    def body(i, carry):
+        for r in range(unroll):
+            fn(i * unroll + r, carry)
+        return carry
+
+    lax.fori_loop(0, n // unroll, body, 0)
 
 
 def kernel(
@@ -41,7 +48,9 @@
     nvb = cells // BLK
     nl = NZ * MEM
     nk = NY * nl
-    hc = cells // 2
+    width = cells // PARTS
+    per_part = nvb // PARTS
+    hz = NZ // 2
 
     def dev(vox, yy, zz):
         return (vox, yy * NZ + zz)
@@ -107,7 +116,7 @@
             core_send[q, xx, g] = par_v[:, pl.ds(col, hdata)].astype(BF16)
         return carry
 
-    loop(NX * NZ, cast_one)
+    loop(NX * NZ, cast_one, 2)
     for cp in loads[1:]:
         cp.wait()
     for s in range(NS):
@@ -143,17 +152,21 @@
             start(core_copy(q, e))
 
     pltpu.make_async_copy(a0.at[v], a1.at[v], a1_rs.at[v]).start()
-    pltpu.make_async_copy(ens.at[:, pl.ds(pl.multiple_of(v * cells, cells), cells)], x1.at[v], x1_rs.at[v]).start()
+    for j in range(PARTS):
+        own = ens.at[:, pl.ds(pl.multiple_of(v * cells + j * width, width), width)]
+        pltpu.make_async_copy(own, x1.at[j, v], x1_rs.at[j, v]).start()
     for d in range(1, NS):
         to = mod(v + d, NS)
         start(rc(a0.at[to], a1.at[v], a1_ss.at[d], a1_rs.at[v], dev(to, y, z)))
 
-    def send_x1(d):
-        to = mod(v + d, NS)
-        start(rc(ens.at[:, pl.ds(pl.multiple_of(to * cells, cells), cells)], x1.at[v], x1_ss.at[d], x1_rs.at[v], dev(to, y, z)))
-
-    for d in X1_EARLY:
-        send_x1(d)
+    def send_x1(j):
+        for d in range(1, NS):
+            to = mod(v + d, NS)
+            src = ens.at[:, pl.ds(pl.multiple_of(to * cells + j * width, width), width)]
+            start(rc(src, x1.at[j, v], x1_ss.at[j, d], x1_rs.at[j, v], dev(to, y, z)))
+
+    for j in range(EARLY):
+        send_x1(j)
 
     @pl.when(home_diag)
     def _():
@@ -187,13 +200,12 @@
                     rs_send[q, e - 1, g] = total.astype(BF16)
                 return carry
 
-            loop(NZ, sum_one)
+            loop(NZ, sum_one, 2)
             if e:
                 start(rc(rs_send.at[q, e - 1], rs_recv.at[q, e - 1], rs_ss.at[q, e - 1], rs_rs.at[q, e - 1], dev(NC * xx + c, y, z)))
 
-    for d in range(1, NS):
-        if d not in X1_EARLY:
-            send_x1(d)
+    for j in range(EARLY, PARTS):
+        send_x1(j)
 
     def forward_a(d):
         g = mod(z + d, NZ)
@@ -203,13 +215,14 @@
         else:
             start(rc(a1.at[g], a2.at[z], az_ss.at[d], az_rs.at[z], dev(v, y, g)))
 
-    def forward_x(d):
-        g = mod(z + d, NZ)
-        arrived(x1.at[g], x1_rs.at[g])
-        if d == 0:
-            pltpu.make_async_copy(x1.at[g], x_all.at[y, z], xz_rs.at[z]).start()
-        else:
-            start(rc(x1.at[g], x_all.at[y, z], xz_ss.at[d], xz_rs.at[z], dev(v, y, g)))
+    def forward_x(j):
+        for d in range(NZ):
+            g = mod(z + d, NZ)
+            arrived(x1.at[j, g], x1_rs.at[j, g])
+            if d == 0:
+                pltpu.make_async_copy(x1.at[j, g], x_all.at[j, y, z], xz_rs.at[j, z]).start()
+            else:
+                start(rc(x1.at[j, g], x_all.at[j, y, z], xz_ss.at[j, d], xz_rs.at[j, z], dev(v, y, g)))
 
     def predict(q):
         for e in range(1, NX):
@@ -222,7 +235,7 @@
             p1[q, g] = total.astype(BF16)
             return carry
 
-        loop(NZ, pred_one)
+        loop(NZ, pred_one, 2)
         pltpu.make_async_copy(p1.at[q, z], p_all.at[q, y, z], pz_rs.at[q, z]).start()
         for d in range(1, NZ):
             g = mod(z + d, NZ)
@@ -237,24 +250,22 @@
 
     ylo, yhi = mod(y + NY - 1, NY), mod(y + 1, NY)
 
-    def spread_x(e):
-        zs = mod(z + NZ - e, NZ)
-        arrived(x_all.at[y, zs], xz_rs.at[zs])
+    def spread_x(j):
+        for e in range(NZ):
+            zs = mod(z + NZ - e, NZ)
+            arrived(x_all.at[j, y, zs], xz_rs.at[j, zs])
         for i, yy in enumerate((yhi, ylo)):
-            start(rc(x_all.at[y, zs], x_all.at[y, zs], xy_ss.at[i, e], xy_rs.at[y, zs], dev(v, yy, z)))
-
-    def relay_x(e):
-        zs = mod(z + NZ - e, NZ)
+            start(rc(x_all.at[j, y], x_all.at[j, y], xy_ss.at[j, i], xy_rs.at[j, y], dev(v, yy, z)))
+
+    def relay_x(j):
         for i, (src, to) in enumerate(((ylo, yhi), (yhi, ylo))):
-            arrived(x_all.at[src, zs], xy_rs.at[src, zs])
-            part = x_all.at[src, zs, :, pl.ds(i * hc, hc)]
-            start(rc(part, part, xr_ss.at[i, e], xr_rs.at[i, zs], dev(v, to, z)))
-
-    def settle_x(e):
-        zs = mod(z + NZ - e, NZ)
-        yo = mod(y + 2, NY)
+            arrived(x_all.at[j, src], xy_rs.at[j, src])
+            part = x_all.at[j, src, pl.ds(i * hz, hz)]
+            start(rc(part, part, xr_ss.at[j, i], xr_rs.at[j, i], dev(v, to, z)))
+
+    def settle_x(j):
         for i in range(2):
-            arrived(x_all.at[yo, zs, :, pl.ds(i * hc, hc)], xr_rs.at[i, zs])
+            arrived(x_all.at[j, mod(y + 2, NY), pl.ds(i * hz, hz)], xr_rs.at[j, i])
 
     def settle_a():
         for e in range(NZ):
@@ -271,7 +282,7 @@
             wt[q * nob + o] = w.astype(BF16)
             return carry
 
-        loop(nob, weight_one)
+        loop(nob, weight_one, 4)
 
     hl = nl // 4
 
@@ -289,7 +300,7 @@
                 m_f[h, pl.ds(o, nl, stride=nob), :] = mom[:, h * 128:(h + 1) * 128]
             return carry
 
-        loop(nob, moment_one)
+        loop(nob, moment_one, 4)
         for k in range(2):
             def cast_m(i, carry):
                 rows = pl.ds(pl.multiple_of((k * hl + i) * 2 * nob, 2 * nob), 2 * nob)
@@ -297,7 +308,7 @@
                     m_all[q, k, v, i, :, h * 128:(h + 1) * 128] = m_f[h, rows, :].astype(BF16)
                 return carry
 
-            loop(hl, cast_m)
+            loop(hl, cast_m, 4)
             mine = m_all.at[q, k, v]
             for i, e in enumerate((1, 3)):
                 start(rc(mine, mine, mx_ss.at[q, k, i], mx_rs.at[q, k, v], dev(mod(v + NC * e, NS), y, z)))
@@ -347,87 +358,93 @@
                     comb[h, rows, :] = com[parity * nvb:(parity + 1) * nvb, h * 128:(h + 1) * 128]
             return carry
 
-        loop(hl, combine_one)
-
-    def centre():
+        loop(hl, combine_one, 4)
+
+    def centre(j):
         def centre_one(b, carry):
             col = pl.ds(pl.multiple_of(b * BLK, BLK), BLK)
-            state = x_all[:, :, :, col].astype(F32).reshape(nk, BLK)
-            xc[b] = (state - jnp.mean(state, axis=0, keepdims=True)).astype(BF16)
+            state = x_all[j, :, :, :, col].astype(F32).reshape(nk, BLK)
+            xc[j * per_part + b] = (state - jnp.mean(state, axis=0, keepdims=True)).astype(BF16)
             return carry
 
-        loop(nvb, centre_one)
-
-    parts = 4
-    per_part = nvb // parts
-    width = per_part * BLK
-
-    def update(q):
-        def update_one(i, carry):
-            b = q * per_part + i
+        loop(per_part, centre_one, 4)
+
+    def update(j):
+        def update_one(b, carry):
             col = pl.ds(pl.multiple_of(b * BLK, BLK), BLK)
-            rows = pl.ds(pl.multiple_of(b * nl, nl), nl)
+            rows = pl.ds(pl.multiple_of((j * per_part + b) * nl, nl), nl)
             left = jnp.concatenate([comb[h, rows, :].astype(BF16) for h in range(2)], axis=1)
-            inc = jnp.dot(left, xc[b], preferred_element_type=F32)
-            own = x_all[y, :, :, col].astype(F32)
-            ost[:, :, col] = (own + inc.reshape(NZ, MEM, BLK) * (1.0 / (nk - 1))).astype(BF16)
+            inc = jnp.dot(left, xc[j * per_part + b], preferred_element_type=F32)
+            own = x_all[j, y, :, :, col].astype(F32)
+            ost[j, :, :, col] = (own + inc.reshape(NZ, MEM, BLK) * (1.0 / (nk - 1))).astype(BF16)
             return carry
 
-        loop(per_part, update_one)
-        src_col = pl.ds(q * width, width)
-        dst_col = pl.ds(pl.multiple_of(v * cells + q * width, width), width)
+        loop(per_part, update_one, 4)
+        dst = out.at[:, pl.ds(pl.multiple_of(v * cells + j * width, width), width)]
         for d in range(NZ):
             zt = mod(z + d, NZ)
-            src, dst = ost.at[zt, :, src_col], out.at[:, dst_col]
+            src = ost.at[j, zt]
             if d == 0:
                 @pl.when(home_diag)
                 def _():
-                    pltpu.make_async_copy(src, dst, o_rs.at[q, v]).start()
+                    pltpu.make_async_copy(src, dst, o_rs.at[j, v]).start()
 
                 @pl.when(jnp.logical_not(home_diag))
                 def _():
-                    rc(src, dst, o_ss.at[q, 0], o_rs.at[q, v], dev(z, y, zt)).start()
+                    rc(src, dst, o_ss.at[j, 0], o_rs.at[j, v], dev(z, y, zt)).start()
             else:
-                start(rc(src, dst, o_ss.at[q, d], o_rs.at[q, v], dev(z, y, zt)))
+                start(rc(src, dst, o_ss.at[j, d], o_rs.at[j, v], dev(z, y, zt)))
 
     for d in range(NZ):
         forward_a(d)
     predict(0)
     predict(1)
-    for d in range(4):
-        forward_x(d)
     spread_p(0)
-    for d in range(4, NZ):
-        forward_x(d)
+    forward_x(0)
     spread_p(1)
+    forward_x(1)
     settle_a()
     weigh(0)
     weigh(1)
-    for e in range(2):
-        spread_x(e)
+    spread_x(0)
+    forward_x(2)
     moments(0)
-    for e in range(2, 4):
-        spread_x(e)
     moments(1)
-    for e in range(4, NZ):
-        spread_x(e)
+    forward_x(3)
+    spread_x(1)
+    relay_x(0)
+    spread_x(2)
+    relay_x(1)
     coeff = spread_coeff()
-    for i, (q, k) in enumerate(((0, 0), (0, 1), (1, 0), (1, 1))):
-        relay_x(2 * i)
-        relay_m(q, k)
-        relay_x(2 * i + 1)
-        finish_m(q, k)
+    relay_m(0, 0)
+    relay_m(0, 1)
+    spread_x(3)
+    finish_m(0, 0)
+    relay_x(2)
+    finish_m(0, 1)
+    settle_x(0)
+    centre(0)
+    relay_m(1, 0)
+    relay_m(1, 1)
+    settle_x(1)
+    centre(1)
+    finish_m(1, 0)
+    finish_m(1, 1)
     settle_m(0, 0)
     settle_m(1, 0)
     combine(coeff, 0)
+    relay_x(3)
     settle_m(0, 1)
     settle_m(1, 1)
     combine(coeff, 1)
-    for e in range(NZ):
-        settle_x(e)
-    centre()
-    for q in range(parts):
-        update(q)
+    update(0)
+    update(1)
+    settle_x(2)
+    centre(2)
+    update(2)
+    settle_x(3)
+    centre(3)
+    update(3)
 
     for cp in sends:
         cp.wait_send()
@@ -444,13 +461,12 @@
 
     @pl.when(jnp.logical_not(home_diag))
     def _():
-        for q in range(parts):
-            rc(ost.at[0, :, pl.ds(0, width)], out.at[:, pl.ds(0, width)], o_ss.at[q, 0], o_rs.at[q, v], partner).wait_send()
-
-    for q in range(parts):
+        for j in range(PARTS):
+            rc(ost.at[j, 0], ost.at[j, 0], o_ss.at[j, 0], o_rs.at[j, v], partner).wait_send()
+
+    for j in range(PARTS):
         for s in range(NS):
-            dst_col = pl.ds(s * cells + q * width, width)
-            arrived(out.at[:, dst_col], o_rs.at[q, s])
+            arrived(out.at[:, pl.ds(s * cells + j * width, width)], o_rs.at[j, s])
 
 
 def local(ensemble, partials, perturb, observed, variance, obs_lists, taper_index, taper_table):
@@ -460,6 +476,7 @@
     nl = NZ * MEM
     nvb = cells // BLK
     hdata = data // 2
+    width = cells // PARTS
     dma = pltpu.SemaphoreType.DMA
     return pl.pallas_call(
         kernel,
@@ -486,31 +503,31 @@
             pltpu.VMEM((4, 16, BLK), BF16),
             pltpu.VMEM((2, NZ, MEM, hdata), BF16),
             pltpu.VMEM((2, NY, NZ, MEM, hdata), BF16),
-            pltpu.VMEM((NS, MEM, cells), BF16),
-            pltpu.VMEM((NY, NZ, MEM, cells), BF16),
+            pltpu.VMEM((PARTS, NS, MEM, width), BF16),
+            pltpu.VMEM((PARTS, NY, NZ, MEM, width), BF16),
             pltpu.VMEM((nvb, NY * nl, BLK), BF16),
             pltpu.VMEM((nob, nl, BLK), BF16),
             pltpu.VMEM((2, nl * nob // 2, 128), F32),
             pltpu.VMEM((2, 2, NS, nl // 4, nob, NY * nl), BF16),
             pltpu.VMEM((2, nvb * nl, 128), F32),
-            pltpu.VMEM((NZ, MEM, cells), BF16),
+            pltpu.VMEM((PARTS, NZ, MEM, width), BF16),
             dma((6,)),
             dma((2, NX)), dma((2, NX)),
             dma((2, NX - 1)), dma((2, NX - 1)),
-            dma((NS,)), dma((NS,)),
+            dma((PARTS, NS)), dma((PARTS, NS)),
             dma((NS,)), dma((NS,)),
             dma((NS,)), dma(()),
             dma((NY,)), dma((4,)),
-            dma((NZ,)), dma((NZ,)),
+            dma((PARTS, NZ)), dma((PARTS, NZ)),
             dma((NZ,)), dma((NZ,)),
             dma((2, NZ)), dma((2, NZ)),
             dma((2, NY)), dma((2, NY)),
-            dma((2, NZ)), dma((NY, NZ)),
-            dma((2, NZ)), dma((2, NZ)),
+            dma((PARTS, 2)), dma((PARTS, NY)),
+            dma((PARTS, 2)), dma((PARTS, 2)),
             dma((2, 2, 2)), dma((2, 2, NS)),
             dma((2, 2, 2)), dma((2, 2, 2)),
             dma((2, 2, 4)), dma((2, 2, NS)),
-            dma((4, NZ)), dma((4, NS)),
+            dma((PARTS, NZ)), dma((PARTS, NS)),
         ],
         compiler_params=pltpu.CompilerParams(
             collective_id=0, has_side_effects=True, vmem_limit_bytes=58 * 1024 * 1024

time: 126 us -> 108 us (0.86); the launches traced: 124 us -> 107 us
  Pallas kernels: 121 us -> 105 us
    pallas_call x1, Pallas kernels: 121 us -> 105 us  [local(): pl.pallas_call(kernel, out_shape=jax.ShapeDtypeStruct(ensemble.shape, BF1...]
where the time goes in v3:
time: 108 us; the launch traced here: 107 us
  Pallas kernels  105 us (97%)
  local copies, waits for them, and re-layouts  2.26 us (2%)
    pallas_call x1, Pallas kernels, local(): pl.pallas_call(kernel, out_shape=jax.ShapeDtypeStruct(ensemble.shape, BF1...  105 us
    unnamed x1, local copies, waits for them, and re-layouts  2.26 us

profile of v3, /device:TPU:1, one launch (start us, length us, event | category | flops | bytes accessed | tf_op | source)
XLA Modules:
  0.0 107.4 jit_solution(5084610995976837687)
XLA Ops:
  0.0 105.1 %update.1 = bf16[8,65536]{1,0:T(8,128)(2,1)} custom-call(bf16[8,65536]{1,0:T(8,128)(2,1)} %ens.1, f32[1,8,131072]{2,1,0:T(8,128)} %par.1, f32[8,16384]{1,0:T(8,128)} %per.1, f32[1,16384]{1,0:T(1,128)} %bitcast.3, f32[8,16,128]{2,1,0:T(8,128)} %bitcast.4, s32[16,64]{1,0:T(8,128)} %lists.1, s32[16,64]{1,0:T(8,128)} %tap_i.1, f32[1,16]{1,0:T(1,128)} %bitcast.5), custom_call_target="tpu_custom_call" | custom-call | flops 900000000 | bytes 8000000 | tf_op jit(solution)/shard_map/update/pallas_call | solution.py:481
  105.1 2.3 %copy.10 = bf16[8,65536]{1,0:T(8,128)(2,1)} copy(bf16[8,65536]{1,0:T(8,128)(2,1)} %update.1) | data formatting | bytes 2097152

commit v4 on v3

--- a/solution.py
+++ b/solution.py
@@ -14,7 +14,6 @@
 BLK = 128
 F32, BF16 = jnp.float32, jnp.bfloat16
 PARTS = 4
-EARLY = 0
 
 
 def loop(n, fn, unroll=1):
@@ -165,9 +164,6 @@
             src = ens.at[:, pl.ds(pl.multiple_of(to * cells + j * width, width), width)]
             start(rc(src, x1.at[j, v], x1_ss.at[j, d], x1_rs.at[j, v], dev(to, y, z)))
 
-    for j in range(EARLY):
-        send_x1(j)
-
     @pl.when(home_diag)
     def _():
         pltpu.make_async_copy(var.at[v], vh, v_rs).start()
@@ -186,7 +182,7 @@
         def _():
             rc(c0, ch.at[c_row], c_ss.at[yy], c_rs.at[c_row], dev(c_to, yy, v)).start()
 
-    for q in range(2):
+    def sums(q):
         for e in (2, 1, 3, 0):
             xx = mod(x + e, NX)
             core_copy(q, e).wait_recv()
@@ -204,8 +200,6 @@
             if e:
                 start(rc(rs_send.at[q, e - 1], rs_recv.at[q, e - 1], rs_ss.at[q, e - 1], rs_rs.at[q, e - 1], dev(NC * xx + c, y, z)))
 
-    for j in range(EARLY, PARTS):
-        send_x1(j)
 
     def forward_a(d):
         g = mod(z + d, NZ)
@@ -395,6 +389,12 @@
             else:
                 start(rc(src, dst, o_ss.at[j, d], o_rs.at[j, v], dev(z, y, zt)))
 
+    sums(0)
+    sums(1)
+    send_x1(0)
+    send_x1(1)
+    send_x1(2)
+    send_x1(3)
     for d in range(NZ):
         forward_a(d)
     predict(0)
@@ -406,38 +406,38 @@
     settle_a()
     weigh(0)
     weigh(1)
+    moments(0)
     spread_x(0)
     forward_x(2)
-    moments(0)
     moments(1)
     forward_x(3)
     spread_x(1)
     relay_x(0)
+    relay_m(0, 0)
+    relay_m(0, 1)
+    finish_m(0, 0)
+    finish_m(0, 1)
+    settle_m(0, 0)
     spread_x(2)
     relay_x(1)
-    coeff = spread_coeff()
-    relay_m(0, 0)
-    relay_m(0, 1)
-    spread_x(3)
-    finish_m(0, 0)
-    relay_x(2)
-    finish_m(0, 1)
-    settle_x(0)
-    centre(0)
     relay_m(1, 0)
     relay_m(1, 1)
-    settle_x(1)
-    centre(1)
     finish_m(1, 0)
     finish_m(1, 1)
-    settle_m(0, 0)
+    coeff = spread_coeff()
+    spread_x(3)
+    relay_x(2)
     settle_m(1, 0)
     combine(coeff, 0)
-    relay_x(3)
     settle_m(0, 1)
     settle_m(1, 1)
     combine(coeff, 1)
+    settle_x(0)
+    centre(0)
     update(0)
+    relay_x(3)
+    settle_x(1)
+    centre(1)
     update(1)
     settle_x(2)
     centre(2)

time: 108 us -> 101 us (0.935)
  Pallas kernels: 105 us -> 98.7 us
    pallas_call x1, Pallas kernels: 105 us -> 98.7 us  [local(): pl.pallas_call(kernel, out_shape=jax.ShapeDtypeStruct(ensemble.shape, BF1...]
where the time goes in v4:
time: 101 us
  Pallas kernels  98.7 us (98%)
  local copies, waits for them, and re-layouts  2.26 us (2%)
    pallas_call x1, Pallas kernels, local(): pl.pallas_call(kernel, out_shape=jax.ShapeDtypeStruct(ensemble.shape, BF1...  98.7 us
    unnamed x1, local copies, waits for them, and re-layouts  2.26 us

profile of v4, /device:TPU:1, one launch (start us, length us, event | category | flops | bytes accessed | tf_op | source)
XLA Modules:
  0.0 101.0 jit_solution(11606067860664215246)
XLA Ops:
  0.0 98.7 %update.1 = bf16[8,65536]{1,0:T(8,128)(2,1)} custom-call(bf16[8,65536]{1,0:T(8,128)(2,1)} %ens.1, f32[1,8,131072]{2,1,0:T(8,128)} %par.1, f32[8,16384]{1,0:T(8,128)} %per.1, f32[1,16384]{1,0:T(1,128)} %bitcast.3, f32[8,16,128]{2,1,0:T(8,128)} %bitcast.4, s32[16,64]{1,0:T(8,128)} %lists.1, s32[16,64]{1,0:T(8,128)} %tap_i.1, f32[1,16]{1,0:T(1,128)} %bitcast.5), custom_call_target="tpu_custom_call" | custom-call | flops 900000000 | bytes 8000000 | tf_op jit(solution)/shard_map/update/pallas_call | solution.py:481
  98.8 2.3 %copy.10 = bf16[8,65536]{1,0:T(8,128)(2,1)} copy(bf16[8,65536]{1,0:T(8,128)(2,1)} %update.1) | data formatting | bytes 2097152

commit v5 on v4

--- a/solution.py
+++ b/solution.py
@@ -427,13 +427,13 @@
     coeff = spread_coeff()
     spread_x(3)
     relay_x(2)
+    settle_x(0)
+    centre(0)
     settle_m(1, 0)
     combine(coeff, 0)
     settle_m(0, 1)
     settle_m(1, 1)
     combine(coeff, 1)
-    settle_x(0)
-    centre(0)
     update(0)
     relay_x(3)
     settle_x(1)

time: 101 us -> 101 us (level)
  no operation moved by 1% of the time
where the time goes in v5:
time: 101 us
  Pallas kernels  98.8 us (98%)
  local copies, waits for them, and re-layouts  2.26 us (2%)
    pallas_call x1, Pallas kernels, local(): pl.pallas_call(kernel, out_shape=jax.ShapeDtypeStruct(ensemble.shape, BF1...  98.8 us
    unnamed x1, local copies, waits for them, and re-layouts  2.26 us

profile of v5, /device:TPU:1, one launch (start us, length us, event | category | flops | bytes accessed | tf_op | source)
XLA Modules:
  0.0 101.0 jit_solution(13056752513259928398)
XLA Ops:
  0.0 98.8 %update.1 = bf16[8,65536]{1,0:T(8,128)(2,1)} custom-call(bf16[8,65536]{1,0:T(8,128)(2,1)} %ens.1, f32[1,8,131072]{2,1,0:T(8,128)} %par.1, f32[8,16384]{1,0:T(8,128)} %per.1, f32[1,16384]{1,0:T(1,128)} %bitcast.3, f32[8,16,128]{2,1,0:T(8,128)} %bitcast.4, s32[16,64]{1,0:T(8,128)} %lists.1, s32[16,64]{1,0:T(8,128)} %tap_i.1, f32[1,16]{1,0:T(1,128)} %bitcast.5), custom_call_target="tpu_custom_call" | custom-call | flops 900000000 | bytes 8000000 | tf_op jit(solution)/shard_map/update/pallas_call | solution.py:481
  98.8 2.3 %copy.10 = bf16[8,65536]{1,0:T(8,128)(2,1)} copy(bf16[8,65536]{1,0:T(8,128)(2,1)} %update.1) | data formatting | bytes 2097152

commit v6 on v4

--- a/solution.py
+++ b/solution.py
@@ -431,11 +431,11 @@
     combine(coeff, 0)
     settle_m(0, 1)
     settle_m(1, 1)
+    relay_x(3)
     combine(coeff, 1)
     settle_x(0)
     centre(0)
     update(0)
-    relay_x(3)
     settle_x(1)
     centre(1)
     update(1)

time: 101 us -> 108 us (1.069)
  Pallas kernels: 98.7 us -> 105 us
    pallas_call x1, Pallas kernels: 98.7 us -> 105 us  [local(): pl.pallas_call(kernel, out_shape=jax.ShapeDtypeStruct(ensemble.shape, BF1...]
where the time goes in v6:
time: 108 us; the launch traced here: 107 us
  Pallas kernels  105 us (97%)
  local copies, waits for them, and re-layouts  2.26 us (2%)
    pallas_call x1, Pallas kernels, local(): pl.pallas_call(kernel, out_shape=jax.ShapeDtypeStruct(ensemble.shape, BF1...  105 us
    unnamed x1, local copies, waits for them, and re-layouts  2.26 us

profile of v6, /device:TPU:1, one launch (start us, length us, event | category | flops | bytes accessed | tf_op | source)
XLA Modules:
  0.0 107.4 jit_solution(9193613300411483835)
XLA Ops:
  0.0 105.1 %update.1 = bf16[8,65536]{1,0:T(8,128)(2,1)} custom-call(bf16[8,65536]{1,0:T(8,128)(2,1)} %ens.1, f32[1,8,131072]{2,1,0:T(8,128)} %par.1, f32[8,16384]{1,0:T(8,128)} %per.1, f32[1,16384]{1,0:T(1,128)} %bitcast.3, f32[8,16,128]{2,1,0:T(8,128)} %bitcast.4, s32[16,64]{1,0:T(8,128)} %lists.1, s32[16,64]{1,0:T(8,128)} %tap_i.1, f32[1,16]{1,0:T(1,128)} %bitcast.5), custom_call_target="tpu_custom_call" | custom-call | flops 900000000 | bytes 8000000 | tf_op jit(solution)/shard_map/update/pallas_call | solution.py:481
  105.1 2.3 %copy.10 = bf16[8,65536]{1,0:T(8,128)(2,1)} copy(bf16[8,65536]{1,0:T(8,128)(2,1)} %update.1) | data formatting | bytes 2097152
